TPU v7x, 128 devices: a whole 4x4x4 slice. The times are simulated.
128 devices in a mesh: dp: 8 (over x, core), mp: 16 (over y, z).
Axes of the slice: x: 4, y: 4, z: 4, core: 2. Of those that a mesh axis runs over, the one named last changes fastest.
Arguments:
- tokens: bfloat16 [512, 8192], P('dp', 'mp'), may hold values from -80 to 80
- frozen_gate_weight: bfloat16 [8192, 28672], P('mp', 'dp'), may hold values from -0.198873782 to 0.198873782
- frozen_up_weight: bfloat16 [8192, 28672], P('mp', 'dp'), may hold values from -0.198873782 to 0.198873782
- frozen_down_weight: bfloat16 [28672, 8192], P('dp', 'mp'), may hold values from -0.28347335 to 0.28347335
- gate_left_factor: bfloat16 [8192, 16], P('mp'), may hold values from -0.0625 to 0.0625
- gate_right_factor: bfloat16 [16, 28672], P(None, 'dp'), may hold values from -0.75 to 0.75
- up_left_factor: bfloat16 [8192, 16], P('mp'), may hold values from -0.0625 to 0.0625
- up_right_factor: bfloat16 [16, 28672], P(None, 'dp'), may hold values from -0.75 to 0.75
- down_left_factor: bfloat16 [28672, 16], P('dp'), may hold values from -0.03125 to 0.03125
- down_right_factor: bfloat16 [16, 8192], P(None, 'mp'), may hold values from -0.75 to 0.75
- gate_column_magnitude: float32 [28672], P('dp'), may hold values from 0.5 to 2
- up_column_magnitude: float32 [28672], P('dp'), may hold values from 0.5 to 2
- down_column_magnitude: float32 [8192], P('mp'), may hold values from 0.5 to 2
- cotangent: bfloat16 [512, 8192], P('dp', 'mp'), may hold values from -80 to 80
Outputs:
- feedforward_output: bfloat16 [512, 8192], P('dp', 'mp')
- token_input_gradient: bfloat16 [512, 8192], P('dp', 'mp')
- gate_magnitude_gradient: float32 [28672], P('dp')
- up_magnitude_gradient: float32 [28672], P('dp')
- down_magnitude_gradient: float32 [8192], P('mp')
- gate_right_factor_gradient: float32 [16, 28672], P(None, 'dp')
- gate_left_factor_gradient: float32 [8192, 16], P('mp')
- up_right_factor_gradient: float32 [16, 28672], P(None, 'dp')
- up_left_factor_gradient: float32 [8192, 16], P('mp')
- down_right_factor_gradient: float32 [16, 8192], P(None, 'mp')
- down_left_factor_gradient: float32 [28672, 16], P('dp')
All inputs are finite; a program needn't handle non-finite values.
Results may differ from a plain program's by a relative error of at most 0.03.
Values may be sent and summed in bfloat16 or wider, within the bound.
A program may use at most 192 MiB of HBM per device.

v0:
```python
import jax
import jax.numpy as jnp
from jax import lax
from jax.sharding import Mesh
from jax.sharding import PartitionSpec as P

MP = ("mp_0", "mp_1")
epsilon = 1e-06


def copy_for_each(shard, axis):
    devices = lax.axis_size(axis)
    return lax.all_to_all(
        jnp.broadcast_to(shard[None], (devices, *shard.shape)), axis, 0, 0, tiled=True
    )


def over_copies(shard, axis):
    return copy_for_each(shard, axis).sum(axis=0)


def packed_total(arrays, axis):
    ends = [0]
    for a in arrays:
        ends.append(ends[-1] + a.size)
    subtotal = over_copies(jnp.concatenate([a.ravel() for a in arrays]), axis)
    return tuple((subtotal[b:e].reshape(a.shape) for a, b, e in zip(arrays, ends, ends[1:])))


def joined_along(tiles, dim):
    dims = list(tiles.shape[1:])
    dims[dim] *= tiles.shape[0]
    return jnp.moveaxis(tiles, 0, dim).reshape(dims)


def collect(shard, axis, dim):
    tiles = copy_for_each(shard, axis)
    return joined_along(tiles, dim)


def taken_together(shard, axis):
    everything = copy_for_each(shard, axis)
    return jnp.sum(everything.astype(jnp.float32), axis=0)


def own_rows(terms, axes):
    subtotal = terms.astype(jnp.bfloat16)
    for axis in axes:
        subtotal = lax.psum_scatter(subtotal, axis, scatter_dimension=0, tiled=True)
    return subtotal.astype(jnp.float32)


def cut_along(shard, dim, devices):
    before, after = (shard.shape[:dim], shard.shape[dim + 1 :])
    return jnp.moveaxis(shard.reshape(*before, devices, -1, *after), dim, 0)


def sent_and_summed(shard, axis, dim):
    tiles = cut_along(shard, dim, lax.axis_size(axis))
    arrived = lax.all_to_all(tiles, axis, split_axis=0, concat_axis=0, tiled=True)
    return arrived.astype(jnp.float32).sum(axis=0)


def side_by_side(arrays, axis, dim, along):
    widths = [a.shape[along] for a in arrays]
    both = jnp.concatenate(arrays, axis=along)
    whole = lax.all_gather(both, axis, axis=dim, tiled=True)
    return tuple(jnp.split(whole, [sum(widths[:k]) for k in range(1, len(widths))], axis=along))


def matrix_product(left_side, right_side):
    return jnp.dot(left_side, right_side, preferred_element_type=jnp.float32)


def matrix_product_right_transposed(left_side, right_side):
    return lax.dot_general(
        left_side, right_side, (((1,), (1,)), ((), ())), preferred_element_type=jnp.float32
    )


def matrix_product_left_transposed(left_side, right_side):
    return lax.dot_general(
        left_side, right_side, (((0,), (0,)), ((), ())), preferred_element_type=jnp.float32
    )


def combine_adapter_columns(weight_matrix, left_factor, right_factor):
    combined_weight = weight_matrix.astype(jnp.float32) + matrix_product(left_factor, right_factor)
    return (
        combined_weight.astype(jnp.bfloat16),
        jnp.sum(combined_weight * combined_weight, axis=0),
    )


def activate(pre_pair, scale_gate, scale_up):
    width = scale_gate.shape[0]
    pre_gate = pre_pair[:, :width]
    pre_up = pre_pair[:, width:]
    gate_act = pre_gate * scale_gate
    up_act = pre_up * scale_up
    sigmoid_gate = jax.nn.sigmoid(gate_act)
    silu_gate = gate_act * sigmoid_gate
    hidden_state = (silu_gate * up_act).astype(jnp.bfloat16)
    return (hidden_state, (pre_gate, pre_up, gate_act, up_act, sigmoid_gate, silu_gate))


def gate_backward(grad_hidden, saved, scale_gate, scale_up):
    pre_gate, pre_up, gate_act, up_act, sigmoid_gate, silu_gate = saved
    grad_gate = grad_hidden * up_act * sigmoid_gate * (1.0 + gate_act * (1.0 - sigmoid_gate))
    grad_up = grad_hidden * silu_gate
    gate_logits = (grad_gate * scale_gate).astype(jnp.bfloat16)
    up_logits = (grad_up * scale_up).astype(jnp.bfloat16)
    return (
        gate_logits,
        up_logits,
        jnp.sum(grad_gate * pre_gate, axis=0),
        jnp.sum(grad_up * pre_up, axis=0),
    )


def per_device(
    tokens,
    frozen_gate_weight,
    frozen_up_weight,
    frozen_down_weight,
    gate_left_factor,
    gate_right_factor,
    up_left_factor,
    up_right_factor,
    down_left_factor,
    down_right_factor,
    gate_column_magnitude,
    up_column_magnitude,
    down_column_magnitude,
    cotangent,
):
    combined_gate_weight, gate_squared_columns = combine_adapter_columns(
        frozen_gate_weight, gate_left_factor, gate_right_factor
    )
    combined_up_weight, up_squared_columns = combine_adapter_columns(
        frozen_up_weight, up_left_factor, up_right_factor
    )
    combined_down_weight, down_squared_columns = combine_adapter_columns(
        frozen_down_weight, down_left_factor, down_right_factor
    )
    gate_squared_columns, up_squared_columns = packed_total(
        (gate_squared_columns, up_squared_columns), MP
    )
    down_squared_columns = over_copies(down_squared_columns, "dp")
    gate_column_norm = jnp.sqrt(gate_squared_columns + epsilon)
    up_column_norm = jnp.sqrt(up_squared_columns + epsilon)
    down_column_norm = jnp.sqrt(down_squared_columns + epsilon)
    scale_gate = gate_column_magnitude / gate_column_norm
    scale_up = up_column_magnitude / up_column_norm
    scale_down = down_column_magnitude / down_column_norm
    collected_rows = collect(tokens, "dp", 0)
    local_rows = collected_rows.shape[0] // lax.axis_size(MP)
    row_start = lax.axis_index(MP) * local_rows
    gate_projection_output, up_projection_output = (
        taken_together(
            matrix_product(collected_rows, gate_left_factor).astype(jnp.bfloat16), MP
        ).astype(jnp.float32),
        taken_together(
            matrix_product(collected_rows, up_left_factor).astype(jnp.bfloat16), MP
        ).astype(jnp.float32),
    )
    gate_projection_output = gate_projection_output.astype(jnp.bfloat16)
    up_projection_output = up_projection_output.astype(jnp.bfloat16)
    row_block = collected_rows
    pre_pair = own_rows(
        jnp.concatenate(
            [
                matrix_product(row_block, combined_gate_weight),
                matrix_product(row_block, combined_up_weight),
            ],
            axis=1,
        ),
        MP,
    )
    hidden_local, saved = activate(pre_pair, scale_gate, scale_up)
    hidden_state_full = lax.all_gather(hidden_local, MP, axis=0, tiled=True)
    row_block = hidden_state_full
    down_preactivation = sent_and_summed(
        matrix_product(row_block, combined_down_weight).astype(jnp.bfloat16), "dp", 0
    )
    feedforward_output = (down_preactivation * scale_down).astype(jnp.bfloat16)
    output_cotangent = cotangent.astype(jnp.float32)
    down_logits = (output_cotangent * scale_down).astype(jnp.bfloat16)
    down_projection_output, mag_down_sum = (
        taken_together(
            matrix_product(hidden_state_full, down_left_factor).astype(jnp.bfloat16), "dp"
        ).astype(jnp.float32),
        taken_together(
            jnp.sum(output_cotangent * down_preactivation, axis=0).astype(jnp.bfloat16), "dp"
        ).astype(jnp.float32),
    )
    down_projection_output = down_projection_output.astype(jnp.bfloat16)
    down_magnitude_gradient = mag_down_sum / down_column_norm
    down_logits_full = collect(down_logits, "dp", 0)
    down_backward_rows = (
        taken_together(
            matrix_product_right_transposed(down_logits_full, down_right_factor).astype(
                jnp.bfloat16
            ),
            MP,
        )
        .astype(jnp.float32)
        .astype(jnp.bfloat16)
    )
    down_right_factor_gradient = matrix_product_left_transposed(
        down_projection_output, down_logits_full
    )
    down_left_factor_gradient = matrix_product_left_transposed(
        hidden_state_full, down_backward_rows
    )
    row_block = down_logits_full
    grad_hidden = sent_and_summed(
        matrix_product_right_transposed(row_block, combined_down_weight).astype(jnp.bfloat16), MP, 0
    )
    gate_logits, up_logits, mag_gate_terms, mag_up_terms = gate_backward(
        grad_hidden, saved, scale_gate, scale_up
    )
    proj_gate_rows = lax.dynamic_slice_in_dim(gate_projection_output, row_start, local_rows, 0)
    proj_up_rows = lax.dynamic_slice_in_dim(up_projection_output, row_start, local_rows, 0)
    gate_backward_rows, up_backward_rows = packed_total(
        (
            matrix_product_right_transposed(gate_logits, gate_right_factor),
            matrix_product_right_transposed(up_logits, up_right_factor),
        ),
        "dp",
    )
    gate_backward_rows, up_backward_rows = side_by_side(
        (gate_backward_rows.astype(jnp.bfloat16), up_backward_rows.astype(jnp.bfloat16)), MP, 0, 1
    )
    (
        gate_magnitude_total,
        up_magnitude_total,
        gate_right_factor_gradient,
        up_right_factor_gradient,
    ) = (
        lax.psum(mag_gate_terms.astype(jnp.bfloat16), MP).astype(jnp.float32),
        lax.psum(mag_up_terms.astype(jnp.bfloat16), MP).astype(jnp.float32),
        lax.psum(
            matrix_product_left_transposed(proj_gate_rows, gate_logits).astype(jnp.bfloat16), MP
        ).astype(jnp.float32),
        lax.psum(
            matrix_product_left_transposed(proj_up_rows, up_logits).astype(jnp.bfloat16), MP
        ).astype(jnp.float32),
    )
    z_gate_full, z_up_full = side_by_side((gate_logits, up_logits), MP, 0, 1)
    gate_magnitude_gradient = gate_magnitude_total / gate_column_norm
    up_magnitude_gradient = up_magnitude_total / up_column_norm
    gate_left_factor_gradient = matrix_product_left_transposed(collected_rows, gate_backward_rows)
    up_left_factor_gradient = matrix_product_left_transposed(collected_rows, up_backward_rows)
    token_input_gradient = sent_and_summed(
        (
            matrix_product_right_transposed(z_gate_full, combined_gate_weight)
            + matrix_product_right_transposed(z_up_full, combined_up_weight)
        ).astype(jnp.bfloat16),
        "dp",
        0,
    ).astype(jnp.bfloat16)
    return (
        feedforward_output,
        token_input_gradient,
        gate_magnitude_gradient,
        up_magnitude_gradient,
        down_magnitude_gradient,
        gate_right_factor_gradient,
        gate_left_factor_gradient,
        up_right_factor_gradient,
        up_left_factor_gradient,
        down_right_factor_gradient,
        down_left_factor_gradient,
    )


def solution(mesh):
    torus = Mesh(mesh.devices.reshape(mesh.shape["dp"], 4, 4), ("dp", "mp_0", "mp_1"))
    in_specs = (
        P("dp", MP),
        P(MP, "dp"),
        P(MP, "dp"),
        P("dp", MP),
        P(MP, None),
        P(None, "dp"),
        P(MP, None),
        P(None, "dp"),
        P("dp", None),
        P(None, MP),
        P("dp"),
        P("dp"),
        P(MP),
        P("dp", MP),
    )
    out_specs = (
        P("dp", MP),
        P("dp", MP),
        P("dp"),
        P("dp"),
        P(MP),
        P(None, "dp"),
        P(MP, None),
        P(None, "dp"),
        P(MP, None),
        P(None, MP),
        P("dp", None),
    )
    return jax.shard_map(
        per_device, mesh=torus, in_specs=in_specs, out_specs=out_specs, check_vma=False
    )
```

profile of v0, /device:TPU:1, one launch (start us, length us, event | category | flops | bytes accessed | tf_op | source)
XLA Modules:
  0.0 435.9 jit_solution(9995394842297708845)
XLA Ops:
  7.2 1.7 broadcast_in_dim.20
  8.9 5.8 %all-to-all-start = ((bf16[8,64,512]{2,1,0:T(8,128)(2,1)}), bf16[8,64,512]{2,1,0:T(8,128)(2,1)S(1)}, u32[]{:S(2)}, u32[]{:S(2)}) async-start(bf16[8,64,512]{2,1,0:T(8,128)(2,1)} %broadcast_in_dim.20), calls=%async_computation | async-start | bytes 1048576 | tf_op jit(solution)/shard_map/all_to_all | solution.py:13
  14.8 5.3 %multiply_reduce_fusion.2 = (f32[3584]{0:T(1024)S(1)}, bf16[512,3584]{1,0:T(8,128)(2,1)}) fusion(bf16[512,16]{0,1:T(8,128)(2,1)} %param.18, bf16[16,3584]{1,0:T(8,128)(2,1)} %param.19, bf16[512,3584]{1,0:T(8,128)(2,1)} %param.15), kind=kOutput, calls=%fused_computation.5 | convolution fusion | flops 67891712 | bytes 7485440 | tf_op jit(solution)/shard_map/dot_general | solution.py:72
  20.1 3.2 multiply_reduce_fusion.1
  23.3 0.9 all-to-all-done
  24.2 4.3 fusion
  28.5 3.9 fusion.1
  32.4 5.5 %pad_maximum_fusion = bf16[512,7168]{0,1:T(8,128)(2,1)} fusion(bf16[512,3584]{0,1:T(8,128)(2,1)} %fusion.1, bf16[512,3584]{0,1:T(8,128)(2,1)S(1)} %fusion), kind=kLoop, calls=%fused_computation | loop fusion | flops 14680064 | bytes 14680064 | tf_op jit(solution)/shard_map/concatenate | solution.py:171
  38.0 10.0 %copy.52 = bf16[512,7168]{1,0:T(8,128)(2,1)} copy(bf16[512,7168]{0,1:T(8,128)(2,1)} %pad_maximum_fusion) | data formatting | bytes 14680064
  48.0 0.7 copy-done.6
  48.7 5.2 %multiply_reduce_fusion = (f32[512]{0:T(512)S(1)}, bf16[3584,512]{1,0:T(8,128)(2,1)}) fusion(bf16[3584,16]{0,1:T(8,128)(2,1)S(1)} %copy-done, bf16[16,512]{1,0:T(8,128)(2,1)S(1)} %copy-done.6, bf16[3584,512]{1,0:T(8,128)(2,1)} %param.17), kind=kOutput, calls=%fused_computation.2 | convolution fusion | flops 67894784 | bytes 7473152 | tf_op jit(solution)/shard_map/dot_general | solution.py:72
  53.9 8.4 %all_to_all.69 = f32[8,1,512]{2,1,0:T(1,128)S(1)} all-to-all(f32[8,1,512]{2,1,0:T(1,128)S(1)} %broadcast_in_dim.22), channel_id=1, replica_groups=mesh['dp'=8,'mp_0'=4,'mp_1'=4] {'dp'}, dimensions={0} | all-to-all | bytes 32768 | tf_op jit(solution)/shard_map/all_to_all | solution.py:13
  62.4 0.9 broadcast_in_dim.23
  63.3 4.0 all-to-all-start.4
  67.3 9.5 %all-to-all-done.4 = bf16[8,64,512]{2,1,0:T(8,128)(2,1)S(1)} async-done(((bf16[8,64,512]{2,1,0:T(8,128)(2,1)}), bf16[8,64,512]{2,1,0:T(8,128)(2,1)S(1)}, u32[]{:S(2)}, u32[]{:S(2)}) %all-to-all-start.4) | async-done | bytes 524320 | tf_op jit(solution)/shard_map/all_to_all | solution.py:13
  76.8 1.0 broadcast_in_dim.21
  77.8 7.8 %all-to-all-start.1 = ((f32[16,1,7168]{2,1,0:T(1,128)}), f32[16,1,7168]{2,1,0:T(1,128)S(1)}, u32[]{:S(2)}, u32[]{:S(2)}) async-start(f32[16,1,7168]{2,1,0:T(1,128)} %broadcast_in_dim.21), calls=%async_computation.1 | async-start | bytes 917504 | tf_op jit(solution)/shard_map/all_to_all | solution.py:13
  85.6 6.1 %convolution_convert_fusion = bf16[512,3584]{1,0:T(8,128)(2,1)} fusion(bf16[512,512]{1,0:T(8,128)(2,1)S(1)} %bitcast.57, bf16[3584,512]{1,0:T(8,128)(2,1)} %get-tuple-element.29), kind=kOutput, calls=%fused_computation.8 | convolution fusion | flops 1880883200 | bytes 7864320 | tf_op jit(solution)/shard_map/dot_general | solution.py:76
  91.7 7.4 %all-to-all-done.1 = f32[16,1,7168]{2,1,0:T(1,128)S(1)} async-done(((f32[16,1,7168]{2,1,0:T(1,128)}), f32[16,1,7168]{2,1,0:T(1,128)S(1)}, u32[]{:S(2)}, u32[]{:S(2)}) %all-to-all-start.1) | async-done | bytes 458784 | tf_op jit(solution)/shard_map/all_to_all | solution.py:13
  99.0 6.0 %all-to-all-start.5 = ((bf16[16,32,3584]{2,1,0:T(8,128)(2,1)}), bf16[16,32,3584]{2,1,0:T(8,128)(2,1)}, u32[]{:S(2)}, u32[]{:S(2)}) async-start(bf16[16,32,3584]{2,1,0:T(8,128)(2,1)} %bitcast.60), calls=%async_computation.5 | async-start | bytes 7340032 | tf_op jit(solution)/shard_map/all_to_all | solution.py:60
  105.1 55.5 %reduce-scatter.7.cloned.1.call-done = bf16[128,7168]{1,0:T(8,128)(2,1)} async-done(((bf16[512,7168]{1,0:T(8,128)(2,1)}), bf16[128,7168]{1,0:T(8,128)(2,1)}) %reduce-scatter.7.cloned.1.call-update) | async-done | bytes 1835024
  161.0 6.8 %all-to-all-done.5 = bf16[16,32,3584]{2,1,0:T(8,128)(2,1)} async-done(((bf16[16,32,3584]{2,1,0:T(8,128)(2,1)}), bf16[16,32,3584]{2,1,0:T(8,128)(2,1)}, u32[]{:S(2)}, u32[]{:S(2)}) %all-to-all-start.5) | async-done | bytes 3670048 | tf_op jit(solution)/shard_map/all_to_all | solution.py:60
  167.8 2.6 convert_reduce_fusion
  170.4 24.2 %reduce-scatter.9.cloned.1.call-done = bf16[32,7168]{1,0:T(8,128)(2,1)} async-done(((bf16[128,7168]{1,0:T(8,128)(2,1)}), bf16[32,7168]{1,0:T(8,128)(2,1)}) %reduce-scatter.9.cloned.1.call-update) | async-done | bytes 458768 | tf_op jit(solution)/shard_map/reduce_scatter | solution.py:49
  194.6 1.1 convert_element_type.124
  195.7 1.0 multiply_reduce_fusion.3
  197.0 0.7 broadcast_in_dim.25
  197.8 5.0 %all-to-all-start.8 = ((bf16[16,512,16]{1,2,0:T(8,128)(2,1)}), bf16[16,512,16]{1,2,0:T(8,128)(2,1)S(1)}, u32[]{:S(2)}, u32[]{:S(2)}) async-start(bf16[16,512,16]{1,2,0:T(8,128)(2,1)} %broadcast_in_dim.25), calls=%async_computation.8 | async-start | bytes 524288 | tf_op jit(solution)/shard_map/all_to_all | solution.py:13
  203.0 7.2 %all-to-all-done.8 = bf16[16,512,16]{1,2,0:T(8,128)(2,1)S(1)} async-done(((bf16[16,512,16]{1,2,0:T(8,128)(2,1)}), bf16[16,512,16]{1,2,0:T(8,128)(2,1)S(1)}, u32[]{:S(2)}, u32[]{:S(2)}) %all-to-all-start.8) | async-done | bytes 262176 | tf_op jit(solution)/shard_map/all_to_all | solution.py:13
  210.3 0.7 broadcast_in_dim.27
  211.0 3.5 all-to-all-start.10
  214.6 7.5 %all-to-all-done.10 = bf16[16,512,16]{1,2,0:T(8,128)(2,1)S(1)} async-done(((bf16[16,512,16]{1,2,0:T(8,128)(2,1)}), bf16[16,512,16]{1,2,0:T(8,128)(2,1)S(1)}, u32[]{:S(2)}, u32[]{:S(2)}) %all-to-all-start.10) | async-done | bytes 262176 | tf_op jit(solution)/shard_map/all_to_all | solution.py:13
  222.2 0.9 convolution_convert_fusion.4
  223.1 0.9 convolution_convert_fusion.3
  224.1 0.8 pad_maximum_fusion.1
  225.2 12.9 %all_to_all.70 = bf16[16,512,16]{1,2,0:T(8,128)(2,1)S(1)} all-to-all(bf16[16,512,16]{1,2,0:T(8,128)(2,1)S(1)} %broadcast_in_dim.29), channel_id=1, replica_groups=mesh['dp'=8,'mp_0'=4,'mp_1'=4] {'mp_0','mp_1'}, dimensions={0} | all-to-all | bytes 524288 | tf_op jit(solution)/shard_map/all_to_all | solution.py:13
  238.7 0.6 broadcast_in_dim.26
  239.4 8.5 %all-to-all-start.9 = ((f32[8,1,1024]{2,1,0:T(1,128)}), f32[8,1,1024]{2,1,0:T(1,128)S(1)}, u32[]{:S(2)}, u32[]{:S(2)}) async-start(f32[8,1,1024]{2,1,0:T(1,128)} %broadcast_in_dim.26), calls=%async_computation.9 | async-start | bytes 65536 | tf_op jit(solution)/shard_map/all_to_all | solution.py:13
  247.8 57.0 %all-reduce = (bf16[3584]{0:T(1024)(128)(2,1)S(1)}, bf16[3584]{0:T(1024)(128)(2,1)S(1)}) all-reduce(bf16[3584]{0:T(1024)(128)(2,1)S(1)} %get-tuple-element.12, bf16[3584]{0:T(1024)(128)(2,1)S(1)} %get-tuple-element.11), channel_id=1, replica_groups=mesh['dp'=8,'mp_0'=4,'mp_1'=4] {'mp_0','mp_1'}, use_global_device_ids=true, to_apply=%region_11.0 | all-reduce | flops 7168 | bytes 28672 | tf_op jit(solution)/shard_map/psum | solution.py:241
  304.9 0.6 convert_divide_fusion
  305.8 15.6 %all_gather.11 = bf16[512,32]{1,0:T(8,128)(2,1)S(1)} all-gather(bf16[32,32]{1,0:T(8,128)(2,1)S(1)} %pad_maximum_fusion.3), channel_id=1, replica_groups=mesh['dp'=8,'mp_0'=4,'mp_1'=4] {'mp_0','mp_1'}, dimensions={0}, use_global_device_ids=true | all-gather | bytes 34816 | tf_op jit(solution)/shard_map/all_gather | solution.py:67
  321.4 0.9 convolution_bitcast_fusion
  322.3 3.1 convolution_convert_fusion.5
  325.4 0.7 broadcast_in_dim.28
  326.1 23.8 %all-to-all-start.11 = ((bf16[8,512,16]{1,2,0:T(8,128)(2,1)}), bf16[8,512,16]{1,2,0:T(8,128)(2,1)S(1)}, u32[]{:S(2)}, u32[]{:S(2)}) async-start(bf16[8,512,16]{1,2,0:T(8,128)(2,1)} %broadcast_in_dim.28), calls=%async_computation.11 | async-start | bytes 262144 | tf_op jit(solution)/shard_map/all_to_all | solution.py:13
  349.9 6.0 %fusion.23 = bf16[512,512]{1,0:T(8,128)(2,1)} fusion(bf16[512,3584]{1,0:T(8,128)(2,1)} %all-gather.3.cloned.1.call-done, bf16[3584,512]{1,0:T(8,128)(2,1)} %get-tuple-element.29), kind=kOutput, calls=%fused_computation.28 | convolution fusion | flops 1879310336 | bytes 7864320 | tf_op jit(solution)/shard_map/dot_general | solution.py:72
  355.9 4.8 %all-to-all-start.2 = ((bf16[8,64,512]{2,1,0:T(8,128)(2,1)}), bf16[8,64,512]{2,1,0:T(8,128)(2,1)S(1)}, u32[]{:S(2)}, u32[]{:S(2)}) async-start(bf16[8,64,512]{2,1,0:T(8,128)(2,1)} %bitcast.3), calls=%async_computation.2 | async-start | bytes 1048576 | tf_op jit(solution)/shard_map/all_to_all | solution.py:60
  360.7 0.8 convolution_bitcast_fusion.1
  361.5 1.6 convert_element_type.146
  363.1 1.6 convert_element_type.151
  364.7 3.3 fusion.45
  368.1 2.1 all-to-all-done.2
  370.3 0.7 fusion.28
  371.4 0.7 reduce.9
  372.1 0.6 reshape.111
  372.8 4.1 all-to-all-start.7
  376.9 28.2 %all-gather.5.cloned.1.call-done = bf16[512,7168]{1,0:T(8,128)(2,1)} async-done(((bf16[32,7168]{1,0:T(8,128)(2,1)}), bf16[512,7168]{1,0:T(8,128)(2,1)}) %all-gather.5.cloned.1.call-update) | async-done | bytes 7340048 | tf_op jit(solution)/shard_map/all_gather | solution.py:67
  405.1 5.4 %fusion.2 = f32[512,512]{1,0:T(8,128)S(1)} fusion(bf16[512,7168]{1,0:T(8,128)(2,1)} %all-gather.5.cloned.1.call-done, bf16[512,3584]{1,0:T(8,128)(2,1)} %get-tuple-element.31), kind=kOutput, calls=%fused_computation.15 | convolution fusion | flops 1879048192 | bytes 8388608 | tf_op jit(solution)/shard_map/dot_general | solution.py:76
  410.5 0.9 copy-done.12
  411.4 2.9 fusion.18
  414.2 4.9 %all-to-all-start.6 = ((bf16[8,64,512]{2,1,0:T(8,128)(2,1)}), bf16[8,64,512]{2,1,0:T(8,128)(2,1)S(1)}, u32[]{:S(2)}, u32[]{:S(2)}) async-start(bf16[8,64,512]{2,1,0:T(8,128)(2,1)} %bitcast.6), calls=%async_computation.6 | async-start | bytes 1048576 | tf_op jit(solution)/shard_map/all_to_all | solution.py:60
  419.2 0.8 fusion.44
  420.6 8.1 %all-to-all-done.6 = bf16[8,64,512]{2,1,0:T(8,128)(2,1)S(1)} async-done(((bf16[8,64,512]{2,1,0:T(8,128)(2,1)}), bf16[8,64,512]{2,1,0:T(8,128)(2,1)S(1)}, u32[]{:S(2)}, u32[]{:S(2)}) %all-to-all-start.6) | async-done | bytes 524320 | tf_op jit(solution)/shard_map/all_to_all | solution.py:60
  428.6 0.7 reduce_sum.175
  (73 shorter events, 3.8 us)
Async XLA Ops:
  7.2 40.8 %copy-start = (bf16[3584,16]{0,1:T(8,128)(2,1)S(1)}, bf16[3584,16]{0,1:T(8,128)(2,1)}, u32[]{:S(2)}) copy-start(bf16[3584,16]{0,1:T(8,128)(2,1)} %param.22) | copy-start | bytes 344068
  8.9 15.3 %all-to-all-start = ((bf16[8,64,512]{2,1,0:T(8,128)(2,1)}), bf16[8,64,512]{2,1,0:T(8,128)(2,1)S(1)}, u32[]{:S(2)}, u32[]{:S(2)}) async-start(bf16[8,64,512]{2,1,0:T(8,128)(2,1)} %broadcast_in_dim.20), calls=%async_computation | async-start | bytes 1048576 | tf_op jit(solution)/shard_map/all_to_all | solution.py:13
  14.7 5.4 %copy-start.3 = (bf16[16,3584]{1,0:T(8,128)(2,1)S(1)}, bf16[16,3584]{1,0:T(8,128)(2,1)}, u32[]{:S(2)}) copy-start(bf16[16,3584]{1,0:T(8,128)(2,1)} %param.21) | copy-start | bytes 344068
  14.7 5.4 %copy-start.5 = (bf16[512,16]{0,1:T(8,128)(2,1)S(1)}, bf16[512,16]{0,1:T(8,128)(2,1)}, u32[]{:S(2)}) copy-start(bf16[512,16]{0,1:T(8,128)(2,1)} %param.20) | copy-start | bytes 49156
  14.7 145.9 %reduce-scatter.7.cloned.1.call-start = ((), (), s32[]{:S(2)}) async-start(), calls=%async_computation.17 | async-start | bytes 9175040
  14.7 5.4 %copy-start.11 = (bf16[512,3584]{1,0:T(8,128)(2,1)S(1)}, bf16[512,3584]{1,0:T(8,128)(2,1)}, u32[]{:S(2)}) copy-start(bf16[512,3584]{1,0:T(8,128)(2,1)} %param.16) | copy-start | bytes 11010052
  24.2 4.3 copy-start.13
  47.9 0.7 copy-start.6
  48.7 13.7 %copy-start.9 = (f32[512]{0:T(512)S(1)}, f32[512]{0:T(512)}, u32[]{:S(2)}) copy-start(f32[512]{0:T(512)} %param.26) | copy-start | bytes 6148
  48.7 13.7 %copy-start.1 = (bf16[64,512]{1,0:T(8,128)(2,1)S(1)}, bf16[64,512]{1,0:T(8,128)(2,1)}, u32[]{:S(2)}) copy-start(bf16[64,512]{1,0:T(8,128)(2,1)} %param.27) | copy-start | bytes 196612
  63.3 13.5 %all-to-all-start.4 = ((bf16[8,64,512]{2,1,0:T(8,128)(2,1)}), bf16[8,64,512]{2,1,0:T(8,128)(2,1)S(1)}, u32[]{:S(2)}, u32[]{:S(2)}) async-start(bf16[8,64,512]{2,1,0:T(8,128)(2,1)} %broadcast_in_dim.23), calls=%async_computation.4 | async-start | bytes 1048576 | tf_op jit(solution)/shard_map/all_to_all | solution.py:13
  77.8 21.2 %all-to-all-start.1 = ((f32[16,1,7168]{2,1,0:T(1,128)}), f32[16,1,7168]{2,1,0:T(1,128)S(1)}, u32[]{:S(2)}, u32[]{:S(2)}) async-start(f32[16,1,7168]{2,1,0:T(1,128)} %broadcast_in_dim.21), calls=%async_computation.1 | async-start | bytes 917504 | tf_op jit(solution)/shard_map/all_to_all | solution.py:13
  99.0 61.9 %copy-start.7 = (f32[3584]{0:T(1024)S(1)}, f32[3584]{0:T(1024)}, u32[]{:S(2)}) copy-start(f32[3584]{0:T(1024)} %param.24) | copy-start | bytes 43012
  99.0 61.9 %copy-start.8 = (f32[3584]{0:T(1024)S(1)}, f32[3584]{0:T(1024)}, u32[]{:S(2)}) copy-start(f32[3584]{0:T(1024)} %param.25) | copy-start | bytes 43012
  99.0 68.8 %all-to-all-start.5 = ((bf16[16,32,3584]{2,1,0:T(8,128)(2,1)}), bf16[16,32,3584]{2,1,0:T(8,128)(2,1)}, u32[]{:S(2)}, u32[]{:S(2)}) async-start(bf16[16,32,3584]{2,1,0:T(8,128)(2,1)} %bitcast.60), calls=%async_computation.5 | async-start | bytes 7340032 | tf_op jit(solution)/shard_map/all_to_all | solution.py:60
  105.0 89.6 %reduce-scatter.9.cloned.1.call-start = ((), (), s32[]{:S(2)}) async-start(), calls=%async_computation.18 | async-start | bytes 2293760 | tf_op jit(solution)/shard_map/reduce_scatter | solution.py:49
  160.6 161.7 %all-gather.3.cloned.1.call-start = ((), (), s32[]{:S(2)}) async-start(), calls=%async_computation.15 | async-start | bytes 3899392 | tf_op jit(solution)/shard_map/all_gather | solution.py:181
  161.0 35.8 %copy-start.4 = (bf16[512,16]{0,1:T(8,128)(2,1)S(1)}, bf16[512,16]{0,1:T(8,128)(2,1)}, u32[]{:S(2)}) copy-start(bf16[512,16]{0,1:T(8,128)(2,1)} %param.18) | copy-start | bytes 49156
  197.0 41.1 %copy-start.2 = (bf16[16,3584]{1,0:T(8,128)(2,1)S(1)}, bf16[16,3584]{1,0:T(8,128)(2,1)}, u32[]{:S(2)}) copy-start(bf16[16,3584]{1,0:T(8,128)(2,1)} %param.19) | copy-start | bytes 344068
  197.8 12.5 %all-to-all-start.8 = ((bf16[16,512,16]{1,2,0:T(8,128)(2,1)}), bf16[16,512,16]{1,2,0:T(8,128)(2,1)S(1)}, u32[]{:S(2)}, u32[]{:S(2)}) async-start(bf16[16,512,16]{1,2,0:T(8,128)(2,1)} %broadcast_in_dim.25), calls=%async_computation.8 | async-start | bytes 524288 | tf_op jit(solution)/shard_map/all_to_all | solution.py:13
  211.0 11.2 %all-to-all-start.10 = ((bf16[16,512,16]{1,2,0:T(8,128)(2,1)}), bf16[16,512,16]{1,2,0:T(8,128)(2,1)S(1)}, u32[]{:S(2)}, u32[]{:S(2)}) async-start(bf16[16,512,16]{1,2,0:T(8,128)(2,1)} %broadcast_in_dim.27), calls=%async_computation.10 | async-start | bytes 524288 | tf_op jit(solution)/shard_map/all_to_all | solution.py:13
  214.5 147.0 %all-reduce.4.cloned.1.call-start = ((), (), s32[]{:S(2)}) async-start(), calls=%async_computation.19 | async-start | bytes 458752 | tf_op jit(solution)/shard_map/psum | solution.py:243
  224.0 181.1 %all-gather.5.cloned.1.call-start = ((), (), s32[]{:S(2)}) async-start(), calls=%async_computation.16 | async-start | bytes 7798784 | tf_op jit(solution)/shard_map/all_gather | solution.py:67
  239.4 66.1 %all-to-all-start.9 = ((f32[8,1,1024]{2,1,0:T(1,128)}), f32[8,1,1024]{2,1,0:T(1,128)S(1)}, u32[]{:S(2)}, u32[]{:S(2)}) async-start(f32[8,1,1024]{2,1,0:T(1,128)} %broadcast_in_dim.26), calls=%async_computation.9 | async-start | bytes 65536 | tf_op jit(solution)/shard_map/all_to_all | solution.py:13
  326.1 29.8 %all-to-all-start.11 = ((bf16[8,512,16]{1,2,0:T(8,128)(2,1)}), bf16[8,512,16]{1,2,0:T(8,128)(2,1)S(1)}, u32[]{:S(2)}, u32[]{:S(2)}) async-start(bf16[8,512,16]{1,2,0:T(8,128)(2,1)} %broadcast_in_dim.28), calls=%async_computation.11 | async-start | bytes 262144 | tf_op jit(solution)/shard_map/all_to_all | solution.py:13
  355.9 14.3 %all-to-all-start.2 = ((bf16[8,64,512]{2,1,0:T(8,128)(2,1)}), bf16[8,64,512]{2,1,0:T(8,128)(2,1)S(1)}, u32[]{:S(2)}, u32[]{:S(2)}) async-start(bf16[8,64,512]{2,1,0:T(8,128)(2,1)} %bitcast.3), calls=%async_computation.2 | async-start | bytes 1048576 | tf_op jit(solution)/shard_map/all_to_all | solution.py:60
  372.8 41.5 %all-to-all-start.7 = ((bf16[8,2,256]{2,1,0:T(2,128)(2,1)}), bf16[8,2,256]{2,1,0:T(2,128)(2,1)S(1)}, u32[]{:S(2)}, u32[]{:S(2)}) async-start(bf16[8,2,256]{2,1,0:T(2,128)(2,1)} %reshape.111), calls=%async_computation.7 | async-start | bytes 16384 | tf_op jit(solution)/shard_map/all_to_all | solution.py:13
  405.1 5.4 %copy-start.10 = (bf16[512,7168]{1,0:T(8,128)(2,1)S(1)}, bf16[512,7168]{1,0:T(8,128)(2,1)}, u32[]{:S(2)}) copy-start(bf16[512,7168]{1,0:T(8,128)(2,1)} %all-gather.5.cloned.1.call-done) | copy-start | bytes 22020100
  405.1 6.3 %copy-start.12 = (bf16[512,3584]{1,0:T(8,128)(2,1)S(1)}, bf16[512,3584]{1,0:T(8,128)(2,1)}, u32[]{:S(2)}) copy-start(bf16[512,3584]{1,0:T(8,128)(2,1)} %get-tuple-element.33) | copy-start | bytes 11010052
  414.2 14.4 %all-to-all-start.6 = ((bf16[8,64,512]{2,1,0:T(8,128)(2,1)}), bf16[8,64,512]{2,1,0:T(8,128)(2,1)S(1)}, u32[]{:S(2)}, u32[]{:S(2)}) async-start(bf16[8,64,512]{2,1,0:T(8,128)(2,1)} %bitcast.6), calls=%async_computation.6 | async-start | bytes 1048576 | tf_op jit(solution)/shard_map/all_to_all | solution.py:60
Sparse Core Ops, SparseCore 0:
  48.1 112.4 reduce-scatter.6
  163.0 31.6 reduce-scatter.8
  197.4 52.6 all-gather.2
  253.9 82.0 all-reduce.3
  338.3 66.7 all-gather.4
where the time goes:
time: 438 us; the launch traced here: 436 us
  waiting for transfers between devices  158 us (36%)
  blocking collectives  93.9 us (21%)
  starting transfers between devices  78.5 us (18%)
  matrix products  54.1 us (12%)
  local copies, waits for them, and re-layouts  19.5 us (4%)
  other arithmetic  18.4 us (4%)
  between operations  14 us (3%)
    all_to_all x8, starting transfers between devices, copy_for_each(): lax.all_to_all(jnp.broadcast_to(shard[None], (devices, *shard.shape)), ax...  62.6 us
    psum x1, blocking collectives, per_device(): lax.psum(mag_gate_terms.astype(jnp.bfloat16), MP).astype(jnp.float32)  57 us
    unnamed x6, waiting for transfers between devices  55.6 us
    all_to_all x8, waiting for transfers between devices, copy_for_each(): lax.all_to_all(jnp.broadcast_to(shard[None], (devices, *shard.shape)), ax...  32.5 us
    dot_general x9, matrix products, matrix_product(): return jnp.dot(left_side, right_side, preferred_element_type=jnp.float32)  31.6 us
    all_gather x1, waiting for transfers between devices, side_by_side(): whole = lax.all_gather(both, axis, axis=dim, tiled=True)  28.2 us
    reduce_scatter x1, waiting for transfers between devices, own_rows(): subtotal = lax.psum_scatter(subtotal, axis, scatter_dimension=0, tiled=True)  24.2 us
    all_to_all x2, blocking collectives, copy_for_each(): lax.all_to_all(jnp.broadcast_to(shard[None], (devices, *shard.shape)), ax...  21.3 us
  transfers between devices with their start and end apart: 16, of which 11 were waited for; matrix products, arithmetic and copies ran while one was open for 14% of the time, Pallas kernels for 0%

commit v1 on v0

--- a/solution.py
+++ b/solution.py
@@ -238,7 +238,7 @@
         gate_right_factor_gradient,
         up_right_factor_gradient,
     ) = (
-        lax.psum(mag_gate_terms.astype(jnp.bfloat16), MP).astype(jnp.float32),
+        lax.psum(lax.psum(mag_gate_terms.astype(jnp.bfloat16), "mp_0"), "mp_1").astype(jnp.float32),
         lax.psum(mag_up_terms.astype(jnp.bfloat16), MP).astype(jnp.float32),
         lax.psum(
             matrix_product_left_transposed(proj_gate_rows, gate_logits).astype(jnp.bfloat16), MP

time: 438 us -> 438 us (level)
  waiting for transfers between devices: 158 us -> 173 us
  blocking collectives: 93.9 us -> 83.4 us
  starting transfers between devices: 78.5 us -> 73.7 us
    all_gather x1, waiting for transfers between devices: 28.2 us -> 43.5 us  [side_by_side(): whole = lax.all_gather(both, axis, axis=dim, tiled=True)]
    psum x1 -> x3, blocking collectives: 57 us -> 44.4 us  [the longest x1 30.5 us: per_device(): lax.psum(mag_up_terms.astype(jnp.bfloat16), MP).astype(jnp.float32)]
    all_to_all x8, starting transfers between devices: 62.6 us -> 57.8 us  [copy_for_each(): lax.all_to_all(jnp.broadcast_to(shard[None], (devices, *shard.shape)), ax...]
where the time goes in v1:
time: 438 us; the launch traced here: 436 us
  waiting for transfers between devices  173 us (39%)
  blocking collectives  83.4 us (19%)
  starting transfers between devices  73.7 us (17%)
  matrix products  54.1 us (12%)
  local copies, waits for them, and re-layouts  19.5 us (4%)
  other arithmetic  18.4 us (4%)
  between operations  14.1 us (3%)
    all_to_all x8, starting transfers between devices, copy_for_each(): lax.all_to_all(jnp.broadcast_to(shard[None], (devices, *shard.shape)), ax...  57.8 us
    unnamed x6, waiting for transfers between devices  55.6 us
    all_gather x1, waiting for transfers between devices, side_by_side(): whole = lax.all_gather(both, axis, axis=dim, tiled=True)  43.5 us
    all_to_all x8, waiting for transfers between devices, copy_for_each(): lax.all_to_all(jnp.broadcast_to(shard[None], (devices, *shard.shape)), ax...  32.5 us
    dot_general x9, matrix products, matrix_product(): return jnp.dot(left_side, right_side, preferred_element_type=jnp.float32)  31.5 us
    psum x1, blocking collectives, per_device(): lax.psum(mag_up_terms.astype(jnp.bfloat16), MP).astype(jnp.float32)  30.5 us
    reduce_scatter x1, waiting for transfers between devices, own_rows(): subtotal = lax.psum_scatter(subtotal, axis, scatter_dimension=0, tiled=True)  24.2 us
    all_to_all x2, blocking collectives, copy_for_each(): lax.all_to_all(jnp.broadcast_to(shard[None], (devices, *shard.shape)), ax...  21.3 us
  transfers between devices with their start and end apart: 16, of which 11 were waited for; matrix products, arithmetic and copies ran while one was open for 14% of the time, Pallas kernels for 0%

profile of v1, /device:TPU:1, one launch (start us, length us, event | category | flops | bytes accessed | tf_op | source)
XLA Modules:
  0.0 435.9 jit_solution(3908132445313161355)
XLA Ops:
  7.2 1.7 broadcast_in_dim.20
  8.9 5.8 %all-to-all-start = ((bf16[8,64,512]{2,1,0:T(8,128)(2,1)}), bf16[8,64,512]{2,1,0:T(8,128)(2,1)S(1)}, u32[]{:S(2)}, u32[]{:S(2)}) async-start(bf16[8,64,512]{2,1,0:T(8,128)(2,1)} %broadcast_in_dim.20), calls=%async_computation | async-start | bytes 1048576 | tf_op jit(solution)/shard_map/all_to_all | solution.py:13
  14.8 5.3 %multiply_reduce_fusion.2 = (f32[3584]{0:T(1024)S(1)}, bf16[512,3584]{1,0:T(8,128)(2,1)}) fusion(bf16[512,16]{0,1:T(8,128)(2,1)} %param.18, bf16[16,3584]{1,0:T(8,128)(2,1)} %param.19, bf16[512,3584]{1,0:T(8,128)(2,1)} %param.15), kind=kOutput, calls=%fused_computation.5 | convolution fusion | flops 67891712 | bytes 7485440 | tf_op jit(solution)/shard_map/dot_general | solution.py:72
  20.1 3.2 multiply_reduce_fusion.1
  23.3 0.9 all-to-all-done
  24.2 4.3 fusion
  28.5 3.9 fusion.1
  32.4 5.5 %pad_maximum_fusion = bf16[512,7168]{0,1:T(8,128)(2,1)} fusion(bf16[512,3584]{0,1:T(8,128)(2,1)} %fusion.1, bf16[512,3584]{0,1:T(8,128)(2,1)S(1)} %fusion), kind=kLoop, calls=%fused_computation | loop fusion | flops 14680064 | bytes 14680064 | tf_op jit(solution)/shard_map/concatenate | solution.py:171
  38.0 10.0 %copy.52 = bf16[512,7168]{1,0:T(8,128)(2,1)} copy(bf16[512,7168]{0,1:T(8,128)(2,1)} %pad_maximum_fusion) | data formatting | bytes 14680064
  48.0 0.7 copy-done.6
  48.7 5.2 %multiply_reduce_fusion = (f32[512]{0:T(512)S(1)}, bf16[3584,512]{1,0:T(8,128)(2,1)}) fusion(bf16[3584,16]{0,1:T(8,128)(2,1)S(1)} %copy-done, bf16[16,512]{1,0:T(8,128)(2,1)S(1)} %copy-done.6, bf16[3584,512]{1,0:T(8,128)(2,1)} %param.17), kind=kOutput, calls=%fused_computation.2 | convolution fusion | flops 67894784 | bytes 7473152 | tf_op jit(solution)/shard_map/dot_general | solution.py:72
  53.9 8.4 %all_to_all.69 = f32[8,1,512]{2,1,0:T(1,128)S(1)} all-to-all(f32[8,1,512]{2,1,0:T(1,128)S(1)} %broadcast_in_dim.22), channel_id=1, replica_groups=mesh['dp'=8,'mp_0'=4,'mp_1'=4] {'dp'}, dimensions={0} | all-to-all | bytes 32768 | tf_op jit(solution)/shard_map/all_to_all | solution.py:13
  62.4 0.9 broadcast_in_dim.23
  63.3 4.0 all-to-all-start.4
  67.3 9.5 %all-to-all-done.4 = bf16[8,64,512]{2,1,0:T(8,128)(2,1)S(1)} async-done(((bf16[8,64,512]{2,1,0:T(8,128)(2,1)}), bf16[8,64,512]{2,1,0:T(8,128)(2,1)S(1)}, u32[]{:S(2)}, u32[]{:S(2)}) %all-to-all-start.4) | async-done | bytes 524320 | tf_op jit(solution)/shard_map/all_to_all | solution.py:13
  76.8 1.0 broadcast_in_dim.21
  77.8 7.8 %all-to-all-start.1 = ((f32[16,1,7168]{2,1,0:T(1,128)}), f32[16,1,7168]{2,1,0:T(1,128)S(1)}, u32[]{:S(2)}, u32[]{:S(2)}) async-start(f32[16,1,7168]{2,1,0:T(1,128)} %broadcast_in_dim.21), calls=%async_computation.1 | async-start | bytes 917504 | tf_op jit(solution)/shard_map/all_to_all | solution.py:13
  85.6 6.1 %convolution_convert_fusion = bf16[512,3584]{1,0:T(8,128)(2,1)} fusion(bf16[512,512]{1,0:T(8,128)(2,1)S(1)} %bitcast.57, bf16[3584,512]{1,0:T(8,128)(2,1)} %get-tuple-element.27), kind=kOutput, calls=%fused_computation.8 | convolution fusion | flops 1880883200 | bytes 7864320 | tf_op jit(solution)/shard_map/dot_general | solution.py:76
  91.7 7.4 %all-to-all-done.1 = f32[16,1,7168]{2,1,0:T(1,128)S(1)} async-done(((f32[16,1,7168]{2,1,0:T(1,128)}), f32[16,1,7168]{2,1,0:T(1,128)S(1)}, u32[]{:S(2)}, u32[]{:S(2)}) %all-to-all-start.1) | async-done | bytes 458784 | tf_op jit(solution)/shard_map/all_to_all | solution.py:13
  99.0 6.0 %all-to-all-start.5 = ((bf16[16,32,3584]{2,1,0:T(8,128)(2,1)}), bf16[16,32,3584]{2,1,0:T(8,128)(2,1)}, u32[]{:S(2)}, u32[]{:S(2)}) async-start(bf16[16,32,3584]{2,1,0:T(8,128)(2,1)} %bitcast.60), calls=%async_computation.5 | async-start | bytes 7340032 | tf_op jit(solution)/shard_map/all_to_all | solution.py:60
  105.1 55.5 %reduce-scatter.7.cloned.1.call-done = bf16[128,7168]{1,0:T(8,128)(2,1)} async-done(((bf16[512,7168]{1,0:T(8,128)(2,1)}), bf16[128,7168]{1,0:T(8,128)(2,1)}) %reduce-scatter.7.cloned.1.call-update) | async-done | bytes 1835024
  161.0 6.8 %all-to-all-done.5 = bf16[16,32,3584]{2,1,0:T(8,128)(2,1)} async-done(((bf16[16,32,3584]{2,1,0:T(8,128)(2,1)}), bf16[16,32,3584]{2,1,0:T(8,128)(2,1)}, u32[]{:S(2)}, u32[]{:S(2)}) %all-to-all-start.5) | async-done | bytes 3670048 | tf_op jit(solution)/shard_map/all_to_all | solution.py:60
  167.8 2.6 convert_reduce_fusion
  170.4 24.2 %reduce-scatter.9.cloned.1.call-done = bf16[32,7168]{1,0:T(8,128)(2,1)} async-done(((bf16[128,7168]{1,0:T(8,128)(2,1)}), bf16[32,7168]{1,0:T(8,128)(2,1)}) %reduce-scatter.9.cloned.1.call-update) | async-done | bytes 458768 | tf_op jit(solution)/shard_map/reduce_scatter | solution.py:49
  194.6 1.1 convert_element_type.124
  195.7 1.0 multiply_reduce_fusion.3
  197.0 0.7 broadcast_in_dim.25
  197.8 5.0 %all-to-all-start.8 = ((bf16[16,512,16]{1,2,0:T(8,128)(2,1)}), bf16[16,512,16]{1,2,0:T(8,128)(2,1)S(1)}, u32[]{:S(2)}, u32[]{:S(2)}) async-start(bf16[16,512,16]{1,2,0:T(8,128)(2,1)} %broadcast_in_dim.25), calls=%async_computation.8 | async-start | bytes 524288 | tf_op jit(solution)/shard_map/all_to_all | solution.py:13
  203.0 7.2 %all-to-all-done.8 = bf16[16,512,16]{1,2,0:T(8,128)(2,1)S(1)} async-done(((bf16[16,512,16]{1,2,0:T(8,128)(2,1)}), bf16[16,512,16]{1,2,0:T(8,128)(2,1)S(1)}, u32[]{:S(2)}, u32[]{:S(2)}) %all-to-all-start.8) | async-done | bytes 262176 | tf_op jit(solution)/shard_map/all_to_all | solution.py:13
  210.3 0.7 broadcast_in_dim.27
  211.0 3.5 all-to-all-start.10
  214.6 7.5 %all-to-all-done.10 = bf16[16,512,16]{1,2,0:T(8,128)(2,1)S(1)} async-done(((bf16[16,512,16]{1,2,0:T(8,128)(2,1)}), bf16[16,512,16]{1,2,0:T(8,128)(2,1)S(1)}, u32[]{:S(2)}, u32[]{:S(2)}) %all-to-all-start.10) | async-done | bytes 262176 | tf_op jit(solution)/shard_map/all_to_all | solution.py:13
  222.2 0.9 convolution_convert_fusion.4
  223.1 0.9 convolution_convert_fusion.3
  224.1 0.8 pad_maximum_fusion.1
  225.2 12.9 %all_to_all.70 = bf16[16,512,16]{1,2,0:T(8,128)(2,1)S(1)} all-to-all(bf16[16,512,16]{1,2,0:T(8,128)(2,1)S(1)} %broadcast_in_dim.29), channel_id=1, replica_groups=mesh['dp'=8,'mp_0'=4,'mp_1'=4] {'mp_0','mp_1'}, dimensions={0} | all-to-all | bytes 524288 | tf_op jit(solution)/shard_map/all_to_all | solution.py:13
  238.7 0.6 broadcast_in_dim.26
  239.4 8.5 %all-to-all-start.9 = ((f32[8,1,1024]{2,1,0:T(1,128)}), f32[8,1,1024]{2,1,0:T(1,128)S(1)}, u32[]{:S(2)}, u32[]{:S(2)}) async-start(f32[8,1,1024]{2,1,0:T(1,128)} %broadcast_in_dim.26), calls=%async_computation.9 | async-start | bytes 65536 | tf_op jit(solution)/shard_map/all_to_all | solution.py:13
  247.8 30.5 %psum.37 = bf16[3584]{0:T(1024)(128)(2,1)S(1)} all-reduce(bf16[3584]{0:T(1024)(128)(2,1)S(1)} %get-tuple-element.11), channel_id=1, replica_groups=mesh['dp'=8,'mp_0'=4,'mp_1'=4] {'mp_0','mp_1'}, use_global_device_ids=true, to_apply=%region_14.0 | all-reduce | flops 3584 | bytes 14336 | tf_op jit(solution)/shard_map/psum | solution.py:242
  278.4 6.4 %psum.35 = bf16[3584]{0:T(1024)(128)(2,1)S(1)} all-reduce(bf16[3584]{0:T(1024)(128)(2,1)S(1)} %get-tuple-element.12), channel_id=1, replica_groups=mesh['dp'=8,'mp_0'=4,'mp_1'=4] {'mp_0'}, use_global_device_ids=true, to_apply=%region_11.0 | all-reduce | flops 3584 | bytes 14336 | tf_op jit(solution)/shard_map/psum | solution.py:241
  284.8 7.5 %psum.36 = bf16[3584]{0:T(1024)(128)(2,1)S(1)} all-reduce(bf16[3584]{0:T(1024)(128)(2,1)S(1)} %psum.35), channel_id=1, replica_groups=mesh['dp'=8,'mp_0'=4,'mp_1'=4] {'mp_1'}, use_global_device_ids=true, to_apply=%region_12.0 | all-reduce | flops 3584 | bytes 14336 | tf_op jit(solution)/shard_map/psum | solution.py:241
  293.3 17.7 %all_gather.11 = bf16[512,32]{1,0:T(8,128)(2,1)S(1)} all-gather(bf16[32,32]{1,0:T(8,128)(2,1)S(1)} %pad_maximum_fusion.3), channel_id=1, replica_groups=mesh['dp'=8,'mp_0'=4,'mp_1'=4] {'mp_0','mp_1'}, dimensions={0}, use_global_device_ids=true | all-gather | bytes 34816 | tf_op jit(solution)/shard_map/all_gather | solution.py:67
  310.9 0.9 convolution_bitcast_fusion
  311.8 3.1 convolution_convert_fusion.5
  314.9 0.7 broadcast_in_dim.28
  315.6 19.0 %all-to-all-start.11 = ((bf16[8,512,16]{1,2,0:T(8,128)(2,1)}), bf16[8,512,16]{1,2,0:T(8,128)(2,1)S(1)}, u32[]{:S(2)}, u32[]{:S(2)}) async-start(bf16[8,512,16]{1,2,0:T(8,128)(2,1)} %broadcast_in_dim.28), calls=%async_computation.11 | async-start | bytes 262144 | tf_op jit(solution)/shard_map/all_to_all | solution.py:13
  334.6 6.0 %fusion.23 = bf16[512,512]{1,0:T(8,128)(2,1)} fusion(bf16[512,3584]{1,0:T(8,128)(2,1)} %all-gather.3.cloned.1.call-done, bf16[3584,512]{1,0:T(8,128)(2,1)} %get-tuple-element.27), kind=kOutput, calls=%fused_computation.28 | convolution fusion | flops 1879310336 | bytes 7864320 | tf_op jit(solution)/shard_map/dot_general | solution.py:72
  340.6 4.8 %all-to-all-start.2 = ((bf16[8,64,512]{2,1,0:T(8,128)(2,1)}), bf16[8,64,512]{2,1,0:T(8,128)(2,1)S(1)}, u32[]{:S(2)}, u32[]{:S(2)}) async-start(bf16[8,64,512]{2,1,0:T(8,128)(2,1)} %bitcast.3), calls=%async_computation.2 | async-start | bytes 1048576 | tf_op jit(solution)/shard_map/all_to_all | solution.py:60
  345.4 0.8 convolution_bitcast_fusion.1
  346.3 1.6 convert_element_type.146
  347.9 1.6 convert_element_type.151
  349.5 3.5 fusion.45
  352.9 2.0 all-to-all-done.2
  355.0 0.7 fusion.28
  356.2 0.7 reduce.9
  357.5 4.1 all-to-all-start.7
  361.6 43.5 %all-gather.5.cloned.1.call-done = bf16[512,7168]{1,0:T(8,128)(2,1)} async-done(((bf16[32,7168]{1,0:T(8,128)(2,1)}), bf16[512,7168]{1,0:T(8,128)(2,1)}) %all-gather.5.cloned.1.call-update) | async-done | bytes 7340048 | tf_op jit(solution)/shard_map/all_gather | solution.py:67
  405.1 5.4 %fusion.2 = f32[512,512]{1,0:T(8,128)S(1)} fusion(bf16[512,7168]{1,0:T(8,128)(2,1)} %all-gather.5.cloned.1.call-done, bf16[512,3584]{1,0:T(8,128)(2,1)} %get-tuple-element.29), kind=kOutput, calls=%fused_computation.15 | convolution fusion | flops 1879048192 | bytes 8388608 | tf_op jit(solution)/shard_map/dot_general | solution.py:76
  410.5 0.9 copy-done.12
  411.4 2.9 fusion.18
  414.2 4.9 %all-to-all-start.6 = ((bf16[8,64,512]{2,1,0:T(8,128)(2,1)}), bf16[8,64,512]{2,1,0:T(8,128)(2,1)S(1)}, u32[]{:S(2)}, u32[]{:S(2)}) async-start(bf16[8,64,512]{2,1,0:T(8,128)(2,1)} %bitcast.6), calls=%async_computation.6 | async-start | bytes 1048576 | tf_op jit(solution)/shard_map/all_to_all | solution.py:60
  419.2 0.8 fusion.44
  420.6 8.1 %all-to-all-done.6 = bf16[8,64,512]{2,1,0:T(8,128)(2,1)S(1)} async-done(((bf16[8,64,512]{2,1,0:T(8,128)(2,1)}), bf16[8,64,512]{2,1,0:T(8,128)(2,1)S(1)}, u32[]{:S(2)}, u32[]{:S(2)}) %all-to-all-start.6) | async-done | bytes 524320 | tf_op jit(solution)/shard_map/all_to_all | solution.py:60
  428.7 0.7 reduce_sum.175
  (75 shorter events, 5.0 us)
Async XLA Ops:
  7.2 40.8 %copy-start = (bf16[3584,16]{0,1:T(8,128)(2,1)S(1)}, bf16[3584,16]{0,1:T(8,128)(2,1)}, u32[]{:S(2)}) copy-start(bf16[3584,16]{0,1:T(8,128)(2,1)} %param.22) | copy-start | bytes 344068
  8.9 15.3 %all-to-all-start = ((bf16[8,64,512]{2,1,0:T(8,128)(2,1)}), bf16[8,64,512]{2,1,0:T(8,128)(2,1)S(1)}, u32[]{:S(2)}, u32[]{:S(2)}) async-start(bf16[8,64,512]{2,1,0:T(8,128)(2,1)} %broadcast_in_dim.20), calls=%async_computation | async-start | bytes 1048576 | tf_op jit(solution)/shard_map/all_to_all | solution.py:13
  14.7 5.4 %copy-start.3 = (bf16[16,3584]{1,0:T(8,128)(2,1)S(1)}, bf16[16,3584]{1,0:T(8,128)(2,1)}, u32[]{:S(2)}) copy-start(bf16[16,3584]{1,0:T(8,128)(2,1)} %param.21) | copy-start | bytes 344068
  14.7 5.4 %copy-start.5 = (bf16[512,16]{0,1:T(8,128)(2,1)S(1)}, bf16[512,16]{0,1:T(8,128)(2,1)}, u32[]{:S(2)}) copy-start(bf16[512,16]{0,1:T(8,128)(2,1)} %param.20) | copy-start | bytes 49156
  14.7 145.9 %reduce-scatter.7.cloned.1.call-start = ((), (), s32[]{:S(2)}) async-start(), calls=%async_computation.17 | async-start | bytes 9175040
  14.7 5.4 %copy-start.11 = (bf16[512,3584]{1,0:T(8,128)(2,1)S(1)}, bf16[512,3584]{1,0:T(8,128)(2,1)}, u32[]{:S(2)}) copy-start(bf16[512,3584]{1,0:T(8,128)(2,1)} %param.16) | copy-start | bytes 11010052
  24.2 4.3 copy-start.13
  47.9 0.7 copy-start.6
  48.7 13.7 %copy-start.9 = (f32[512]{0:T(512)S(1)}, f32[512]{0:T(512)}, u32[]{:S(2)}) copy-start(f32[512]{0:T(512)} %param.26) | copy-start | bytes 6148
  48.7 13.7 %copy-start.1 = (bf16[64,512]{1,0:T(8,128)(2,1)S(1)}, bf16[64,512]{1,0:T(8,128)(2,1)}, u32[]{:S(2)}) copy-start(bf16[64,512]{1,0:T(8,128)(2,1)} %param.27) | copy-start | bytes 196612
  63.3 13.5 %all-to-all-start.4 = ((bf16[8,64,512]{2,1,0:T(8,128)(2,1)}), bf16[8,64,512]{2,1,0:T(8,128)(2,1)S(1)}, u32[]{:S(2)}, u32[]{:S(2)}) async-start(bf16[8,64,512]{2,1,0:T(8,128)(2,1)} %broadcast_in_dim.23), calls=%async_computation.4 | async-start | bytes 1048576 | tf_op jit(solution)/shard_map/all_to_all | solution.py:13
  77.8 21.2 %all-to-all-start.1 = ((f32[16,1,7168]{2,1,0:T(1,128)}), f32[16,1,7168]{2,1,0:T(1,128)S(1)}, u32[]{:S(2)}, u32[]{:S(2)}) async-start(f32[16,1,7168]{2,1,0:T(1,128)} %broadcast_in_dim.21), calls=%async_computation.1 | async-start | bytes 917504 | tf_op jit(solution)/shard_map/all_to_all | solution.py:13
  99.0 61.9 %copy-start.7 = (f32[3584]{0:T(1024)S(1)}, f32[3584]{0:T(1024)}, u32[]{:S(2)}) copy-start(f32[3584]{0:T(1024)} %param.24) | copy-start | bytes 43012
  99.0 61.9 %copy-start.8 = (f32[3584]{0:T(1024)S(1)}, f32[3584]{0:T(1024)}, u32[]{:S(2)}) copy-start(f32[3584]{0:T(1024)} %param.25) | copy-start | bytes 43012
  99.0 68.8 %all-to-all-start.5 = ((bf16[16,32,3584]{2,1,0:T(8,128)(2,1)}), bf16[16,32,3584]{2,1,0:T(8,128)(2,1)}, u32[]{:S(2)}, u32[]{:S(2)}) async-start(bf16[16,32,3584]{2,1,0:T(8,128)(2,1)} %bitcast.60), calls=%async_computation.5 | async-start | bytes 7340032 | tf_op jit(solution)/shard_map/all_to_all | solution.py:60
  105.0 89.6 %reduce-scatter.9.cloned.1.call-start = ((), (), s32[]{:S(2)}) async-start(), calls=%async_computation.18 | async-start | bytes 2293760 | tf_op jit(solution)/shard_map/reduce_scatter | solution.py:49
  160.6 151.2 %all-gather.3.cloned.1.call-start = ((), (), s32[]{:S(2)}) async-start(), calls=%async_computation.15 | async-start | bytes 3899392 | tf_op jit(solution)/shard_map/all_gather | solution.py:181
  161.0 35.8 %copy-start.4 = (bf16[512,16]{0,1:T(8,128)(2,1)S(1)}, bf16[512,16]{0,1:T(8,128)(2,1)}, u32[]{:S(2)}) copy-start(bf16[512,16]{0,1:T(8,128)(2,1)} %param.18) | copy-start | bytes 49156
  197.0 41.1 %copy-start.2 = (bf16[16,3584]{1,0:T(8,128)(2,1)S(1)}, bf16[16,3584]{1,0:T(8,128)(2,1)}, u32[]{:S(2)}) copy-start(bf16[16,3584]{1,0:T(8,128)(2,1)} %param.19) | copy-start | bytes 344068
  197.8 12.5 %all-to-all-start.8 = ((bf16[16,512,16]{1,2,0:T(8,128)(2,1)}), bf16[16,512,16]{1,2,0:T(8,128)(2,1)S(1)}, u32[]{:S(2)}, u32[]{:S(2)}) async-start(bf16[16,512,16]{1,2,0:T(8,128)(2,1)} %broadcast_in_dim.25), calls=%async_computation.8 | async-start | bytes 524288 | tf_op jit(solution)/shard_map/all_to_all | solution.py:13
  211.0 11.2 %all-to-all-start.10 = ((bf16[16,512,16]{1,2,0:T(8,128)(2,1)}), bf16[16,512,16]{1,2,0:T(8,128)(2,1)S(1)}, u32[]{:S(2)}, u32[]{:S(2)}) async-start(bf16[16,512,16]{1,2,0:T(8,128)(2,1)} %broadcast_in_dim.27), calls=%async_computation.10 | async-start | bytes 524288 | tf_op jit(solution)/shard_map/all_to_all | solution.py:13
  214.5 131.7 %all-reduce.3.cloned.1.call-start = ((), (), s32[]{:S(2)}) async-start(), calls=%async_computation.19 | async-start | bytes 458752 | tf_op jit(solution)/shard_map/psum | solution.py:243
  224.0 181.1 %all-gather.5.cloned.1.call-start = ((), (), s32[]{:S(2)}) async-start(), calls=%async_computation.16 | async-start | bytes 7798784 | tf_op jit(solution)/shard_map/all_gather | solution.py:67
  239.4 53.6 %all-to-all-start.9 = ((f32[8,1,1024]{2,1,0:T(1,128)}), f32[8,1,1024]{2,1,0:T(1,128)S(1)}, u32[]{:S(2)}, u32[]{:S(2)}) async-start(f32[8,1,1024]{2,1,0:T(1,128)} %broadcast_in_dim.26), calls=%async_computation.9 | async-start | bytes 65536 | tf_op jit(solution)/shard_map/all_to_all | solution.py:13
  315.6 25.1 %all-to-all-start.11 = ((bf16[8,512,16]{1,2,0:T(8,128)(2,1)}), bf16[8,512,16]{1,2,0:T(8,128)(2,1)S(1)}, u32[]{:S(2)}, u32[]{:S(2)}) async-start(bf16[8,512,16]{1,2,0:T(8,128)(2,1)} %broadcast_in_dim.28), calls=%async_computation.11 | async-start | bytes 262144 | tf_op jit(solution)/shard_map/all_to_all | solution.py:13
  340.6 14.3 %all-to-all-start.2 = ((bf16[8,64,512]{2,1,0:T(8,128)(2,1)}), bf16[8,64,512]{2,1,0:T(8,128)(2,1)S(1)}, u32[]{:S(2)}, u32[]{:S(2)}) async-start(bf16[8,64,512]{2,1,0:T(8,128)(2,1)} %bitcast.3), calls=%async_computation.2 | async-start | bytes 1048576 | tf_op jit(solution)/shard_map/all_to_all | solution.py:60
  357.5 56.8 %all-to-all-start.7 = ((bf16[8,2,256]{2,1,0:T(2,128)(2,1)}), bf16[8,2,256]{2,1,0:T(2,128)(2,1)S(1)}, u32[]{:S(2)}, u32[]{:S(2)}) async-start(bf16[8,2,256]{2,1,0:T(2,128)(2,1)} %reshape.111), calls=%async_computation.7 | async-start | bytes 16384 | tf_op jit(solution)/shard_map/all_to_all | solution.py:13
  405.1 5.4 %copy-start.10 = (bf16[512,7168]{1,0:T(8,128)(2,1)S(1)}, bf16[512,7168]{1,0:T(8,128)(2,1)}, u32[]{:S(2)}) copy-start(bf16[512,7168]{1,0:T(8,128)(2,1)} %all-gather.5.cloned.1.call-done) | copy-start | bytes 22020100
  405.1 6.3 %copy-start.12 = (bf16[512,3584]{1,0:T(8,128)(2,1)S(1)}, bf16[512,3584]{1,0:T(8,128)(2,1)}, u32[]{:S(2)}) copy-start(bf16[512,3584]{1,0:T(8,128)(2,1)} %get-tuple-element.31) | copy-start | bytes 11010052
  414.2 14.4 %all-to-all-start.6 = ((bf16[8,64,512]{2,1,0:T(8,128)(2,1)}), bf16[8,64,512]{2,1,0:T(8,128)(2,1)S(1)}, u32[]{:S(2)}, u32[]{:S(2)}) async-start(bf16[8,64,512]{2,1,0:T(8,128)(2,1)} %bitcast.6), calls=%async_computation.6 | async-start | bytes 1048576 | tf_op jit(solution)/shard_map/all_to_all | solution.py:60
Sparse Core Ops, SparseCore 0:
  48.1 112.4 reduce-scatter.6
  163.0 31.6 reduce-scatter.8
  197.4 52.6 all-gather.2
  253.9 82.0 all-reduce.2
  338.3 66.7 all-gather.4
